TPU v7x, 128 devices: a whole 4x4x4 slice. The times are simulated.
128 devices in a mesh: dp: 32 (over x, z, core), seq: 4 (over y).
Axes of the slice: x: 4, y: 4, z: 4, core: 2. Of those that a mesh axis runs over, the one named last changes fastest.
Arguments:
- rewards: float32 [65536, 4096], P(('dp', 'seq')), may hold values from -21 to 21
- lengths: int32 [65536], P(('dp', 'seq')), may hold values from 512 to 4096
- prompt_ids: int32 [65536], P(('dp', 'seq')), may hold values from 0 to 4095, as said below
Outputs:
- advantage: float32 [65536, 4096], P(('dp', 'seq'))
- prompt_mean: float32 [4096], P('dp')
- prompt_var: float32 [4096], P('dp')
Inputs may be any that keep to these rules, and one draw needn't show every extreme that they name: `prompt_ids`: each prompt id is named by exactly 16 completions. Every aligned block of 512 completions holds exactly 16 completions of the prompts o * 128 to (o + 1) * 128 - 1, for every o.
All inputs are finite; a program needn't handle non-finite values.
Results may differ from a plain program's by a relative error of at most 0.00011.
Values sent between devices are 32-bit elements; how exact they have to be, the bound alone decides.
No kernel may reach another device: no remote copies, remote signals or barrier semaphores. Data moves between devices by JAX's collectives and lax.ppermute only.
A program may use at most 64 MiB of HBM per device.

v0:
```python
import jax
import jax.numpy as jnp
from jax import lax
from jax.sharding import Mesh
from jax.sharding import PartitionSpec as P

P_DEV = 128
DP = ("dp_0", "dp_1", "dp_2")
DP_SEQ = ("dp_0", "dp_1", "dp_2", "seq")


EPSILON = 1e-06


def gathered_once(shard, axis):
    leaves = jax.tree.leaves(shard)
    turns = sorted(range(len(leaves)), key=lambda k: -leaves[k].size)
    width = (1, *leaves[turns[0]].shape)[-1]
    lines = [
        jnp.pad(leaves[k].reshape(-1), (0, -leaves[k].size % width)).reshape(-1, width)
        for k in turns
    ]
    both, at, found = (lax.all_gather(jnp.concatenate(lines), axis), 0, {})
    for k, line in zip(turns, lines):
        slab = both[:, at : at + len(line)].reshape(len(both), -1)
        found[k] = slab[:, : leaves[k].size].reshape(-1, *leaves[k].shape)
        at += len(line)
    numbers = iter(range(len(leaves)))
    return jax.tree.map(lambda _: found[next(numbers)], shard)


def merged_by_axis(shard, axes, combine):
    for axis in axes:
        pieces = gathered_once(shard, axis)
        shard = jax.tree.map(lambda part: part[0], pieces)
        for k in range(1, lax.axis_size(axis)):
            shard = combine(shard, jax.tree.map(lambda part: part[k], pieces))
    return shard


def welford_join(earlier, later):
    count_one, mean_one, spread_one = earlier
    count_two, mean_two, spread_two = later
    count_all = count_one + count_two
    share = count_two / jnp.maximum(count_all, 1.0)
    delta = mean_two - mean_one
    return (
        count_all,
        mean_one + delta * share,
        spread_one + spread_two + delta * delta * count_one * share,
    )


def select_dot(left, right):
    return jnp.dot(left, right, precision=lax.Precision.HIGHEST, preferred_element_type=jnp.float32)


def row_statistics(rewards, lengths, columns):
    valid = columns[None, :] < lengths[:, None]
    row_count = jnp.sum(valid.astype(jnp.float32), axis=1)
    row_mean = jnp.sum(jnp.where(valid, rewards, 0.0), axis=1) / jnp.maximum(row_count, 1.0)
    deviation = jnp.where(valid, rewards - row_mean[:, None], 0.0)
    row_spread = jnp.sum(deviation * deviation, axis=1)
    return (valid, row_count, row_mean, row_spread)


def group_triples(one_hot, row_count, row_mean, row_spread):
    part_count = select_dot(row_count, one_hot)
    part_mean = select_dot(row_count * row_mean, one_hot) / jnp.maximum(part_count, 1.0)
    slot_part = select_dot(one_hot, part_mean)
    offset = row_mean - slot_part
    part_spread = select_dot(row_spread + row_count * offset * offset, one_hot)
    return (part_count, part_mean, part_spread)


def body(rewards, lengths, prompt_ids):
    samples, width = rewards.shape
    owner_count = lax.axis_size(DP)
    columns = jnp.arange(width, dtype=jnp.int32)
    first_prompt = lax.axis_index(DP) * P_DEV
    valid, row_count, row_mean, row_spread = row_statistics(rewards, lengths, columns)
    every_range = jnp.arange(P_DEV * owner_count, dtype=jnp.int32)
    one_hot = (prompt_ids[:, None] == every_range[None, :]).astype(jnp.float32)
    part_count, part_mean, part_spread = group_triples(one_hot, row_count, row_mean, row_spread)
    count_all, mean_all, spread = merged_by_axis(
        (part_count, part_mean, part_spread), DP_SEQ, welford_join
    )
    var_all = spread / count_all
    inv_std = lax.rsqrt(var_all + EPSILON)
    own_mean = select_dot(one_hot, mean_all)
    own_scale = select_dot(one_hot, inv_std)
    advantage = jnp.where(valid, (rewards - own_mean[:, None]) * own_scale[:, None], 0.0)
    prompt_mean = lax.dynamic_slice_in_dim(mean_all, first_prompt, P_DEV)
    prompt_var = lax.dynamic_slice_in_dim(var_all, first_prompt, P_DEV)
    return (advantage, prompt_mean, prompt_var)


def solution(mesh):
    split = Mesh(mesh.devices.reshape(4, 4, 2, mesh.shape["seq"]), ("dp_0", "dp_1", "dp_2", "seq"))
    placed = (P(DP_SEQ, None), P(DP_SEQ), P(DP_SEQ))
    return jax.shard_map(
        body,
        mesh=split,
        in_specs=placed,
        out_specs=(P(DP_SEQ, None), P(DP), P(DP)),
        check_vma=False,
    )
```

profile of v0, /device:TPU:1, one launch (start us, length us, event | category | flops | bytes accessed | tf_op | source)
XLA Modules:
  0.0 75.5 jit_solution(2182528530968126783)
XLA Ops:
  0.6 0.0 copy-start.1
  0.6 0.0 copy-start
  0.7 0.0 copy-start.2
  0.7 5.8 %convert_reduce_fusion = (f32[512]{0:T(512)S(1)}, f32[512]{0:T(512)S(1)}) fusion(s32[512]{0:T(512)} %param.4, f32[512,4096]{1,0:T(8,128)} %param.3), kind=kLoop, calls=%fused_computation.3 | loop fusion | flops 10484736 | bytes 8394752 | tf_op jit(solution)/shard_map/reduce_sum | solution.py:60
  6.5 0.0 copy-done.1
  6.5 0.0 copy-done
  6.5 2.2 %multiply_reduce_fusion = f32[512]{0:T(512)S(1)} fusion(f32[512,4096]{1,0:T(8,128)S(1)} %copy-done, f32[512]{0:T(512)S(1)} %get-tuple-element.29, s32[512]{0:T(512)S(1)} %copy-done.1), kind=kLoop, calls=%fused_computation.1 | loop fusion | flops 10485248 | bytes 8394752 | tf_op jit(solution)/shard_map/reduce_sum | solution.py:63
  8.7 0.0 copy-done.2
  8.7 2.8 %fusion.4 = f32[1,4096]{1,0:T(1,128)S(1)} fusion(f32[512,1]{0,1:T(1,128)S(1)} %bitcast.341, s32[512]{0:T(512)S(1)} %copy-done.2), kind=kOutput, calls=%fused_computation.9 | convolution fusion | flops 27262976 | bytes 20480 | tf_op jit(solution)/shard_map/dot_general | solution.py:55
  11.5 2.8 %fusion.5 = f32[1,4096]{1,0:T(1,128)S(1)} fusion(f32[512,1]{0,1:T(1,128)S(1)} %bitcast.333, s32[512]{0:T(512)S(1)} %copy-done.2), kind=kOutput, calls=%fused_computation.10 | convolution fusion | flops 27262976 | bytes 20480 | tf_op jit(solution)/shard_map/dot_general | solution.py:55
  14.3 3.9 %fusion.3 = f32[1,512]{1,0:T(1,128)S(1)} fusion(f32[4096,1]{0,1:T(1,128)S(1)} %bitcast.331, s32[512]{0:T(512)S(1)} %copy-done.2), kind=kOutput, calls=%fused_computation.8 | convolution fusion | flops 27262976 | bytes 20480 | tf_op jit(solution)/shard_map/dot_general | solution.py:55
  18.2 2.8 %fusion.2 = f32[1,4096]{1,0:T(1,128)S(1)} fusion(f32[512,1]{0,1:T(1,128)S(1)} %bitcast.339, s32[512]{0:T(512)S(1)} %copy-done.2), kind=kOutput, calls=%fused_computation.7 | convolution fusion | flops 27262976 | bytes 20480 | tf_op jit(solution)/shard_map/dot_general | solution.py:55
  20.9 0.1 maximum_bitcast_fusion
  21.0 11.0 %all-gather.4 = f32[4,3,4096]{2,1,0:T(4,128)S(1)} all-gather(f32[1,3,4096]{2,1,0:T(4,128)S(1)} %maximum_bitcast_fusion), channel_id=2, replica_groups=mesh['dp_0'=4,'dp_1'=4,'dp_2'=2,'seq'=4] {'dp_0'}, dimensions={0}, use_global_device_ids=true | all-gather | bytes 245760 | tf_op jit(solution)/shard_map/all_gather | solution.py:23
  32.0 0.1 multiply_add_fusion.7
  32.1 0.2 fusion.25
  32.4 10.8 %all-gather.5 = f32[4,3,4096]{2,1,0:T(4,128)S(1)} all-gather(f32[1,3,4096]{2,1,0:T(4,128)S(1)} %maximum_bitcast_fusion.1), channel_id=3, replica_groups=mesh['dp_0'=4,'dp_1'=4,'dp_2'=2,'seq'=4] {'dp_1'}, dimensions={0}, use_global_device_ids=true | all-gather | bytes 245760 | tf_op jit(solution)/shard_map/all_gather | solution.py:23
  43.2 0.1 multiply_add_fusion.4
  43.3 0.2 fusion.16
  43.6 7.6 %all-gather.6 = f32[2,3,4096]{2,1,0:T(4,128)S(1)} all-gather(f32[1,3,4096]{2,1,0:T(4,128)S(1)} %maximum_bitcast_fusion.2), channel_id=4, replica_groups=mesh['dp_0'=4,'dp_1'=4,'dp_2'=2,'seq'=4] {'dp_2'}, dimensions={0}, use_global_device_ids=true | all-gather | bytes 147456 | tf_op jit(solution)/shard_map/all_gather | solution.py:23
  51.3 0.1 multiply_add_fusion.3
  51.3 0.1 fusion.13
  51.4 10.6 %all-gather.7 = f32[4,3,4096]{2,1,0:T(4,128)S(1)} all-gather(f32[1,3,4096]{2,1,0:T(4,128)S(1)} %maximum_bitcast_fusion.3), channel_id=5, replica_groups=mesh['dp_0'=4,'dp_1'=4,'dp_2'=2,'seq'=4] {'seq'}, dimensions={0}, use_global_device_ids=true | all-gather | bytes 245760 | tf_op jit(solution)/shard_map/all_gather | solution.py:23
  62.0 0.1 fusion.45
  62.2 3.9 %fusion = f32[1,512]{1,0:T(1,128)S(1)} fusion(f32[4096,1]{0,1:T(1,128)S(1)} %bitcast.335, s32[512]{0:T(512)S(1)} %copy-done.2), kind=kOutput, calls=%fused_computation.5 | convolution fusion | flops 27262976 | bytes 20480 | tf_op jit(solution)/shard_map/dot_general | solution.py:55
  66.0 0.6 dynamic_slice.7
  66.6 0.6 dynamic_slice.6
  67.2 3.9 %fusion.1 = f32[1,512]{1,0:T(1,128)S(1)} fusion(f32[4096,1]{0,1:T(1,128)S(1)} %bitcast.334, s32[512]{0:T(512)S(1)} %copy-done.2), kind=kOutput, calls=%fused_computation.6 | convolution fusion | flops 27262976 | bytes 20480 | tf_op jit(solution)/shard_map/dot_general | solution.py:55
  71.1 4.4 %multiply_select_fusion = f32[512,4096]{1,0:T(8,128)} fusion(f32[512,4096]{1,0:T(8,128)S(1)} %copy-done, f32[512]{0:T(512)S(1)} %bitcast.337, f32[512]{0:T(512)S(1)} %bitcast.338, s32[512]{0:T(512)S(1)} %copy-done.1), kind=kLoop, calls=%fused_computation | loop fusion | flops 8388608 | bytes 16783360 | tf_op jit(solution)/shard_map/jit(_where)/select_n | solution.py:92
  (7 shorter events, 0.2 us)
Async XLA Ops:
  0.6 5.9 %copy-start.1 = (s32[512]{0:T(512)S(1)}, s32[512]{0:T(512)}, u32[]{:S(2)}) copy-start(s32[512]{0:T(512)} %param.4) | copy-start | bytes 6148
  0.6 5.9 %copy-start = (f32[512,4096]{1,0:T(8,128)S(1)}, f32[512,4096]{1,0:T(8,128)}, u32[]{:S(2)}) copy-start(f32[512,4096]{1,0:T(8,128)} %param.3) | copy-start | bytes 25165828
  0.7 8.0 %copy-start.2 = (s32[512]{0:T(512)S(1)}, s32[512]{0:T(512)}, u32[]{:S(2)}) copy-start(s32[512]{0:T(512)} %param.5) | copy-start | bytes 6148
where the time goes:
time: 77 us; the launch traced here: 75.5 us
  blocking collectives  40 us (52%)
  matrix products  19.9 us (26%)
  other arithmetic  13.6 us (18%)
  local copies, waits for them, and re-layouts  1.19 us (2%)
  between operations  0.78 us (1%)
    all_gather x4, blocking collectives, gathered_once(): both, at, found = (lax.all_gather(jnp.concatenate(lines), axis), 0, {})  40 us
    dot_general x6, matrix products, select_dot(): jnp.dot(left, right, precision=lax.Precision.HIGHEST, preferred_element_t...  19.9 us
    reduce_sum x1, other arithmetic, row_statistics(): row_count = jnp.sum(valid.astype(jnp.float32), axis=1)  5.8 us
    select_n x1, other arithmetic, body(): jnp.where(valid, (rewards - own_mean[:, None]) * own_scale[:, None], 0.0)  4.43 us
    reduce_sum x1, other arithmetic, row_statistics(): row_spread = jnp.sum(deviation * deviation, axis=1)  2.19 us

commit v1 on v0

v1 whole, which is shorter than its diff:
```python
import jax
import jax.numpy as jnp
from jax import lax
from jax.experimental import pallas as pl
from jax.experimental.pallas import tpu as pltpu
from jax.sharding import Mesh
from jax.sharding import PartitionSpec as P

P_DEV = 128
OWNERS = 32
SEG = 16
LANES = 128
DP = ("dp_0", "dp_1", "dp_2")
DP_SEQ = ("dp_0", "dp_1", "dp_2", "seq")
CHIPS = ("dp_0", "dp_1", "seq")
EPSILON = 1e-06
MIB = 1024 * 1024
SURE = 4

PARTS = 4
VALUES = 4
ROWS_MSG = PARTS * VALUES


def lane_of(shape):
    return lax.broadcasted_iota(jnp.int32, shape, len(shape) - 1)


def spin(x, k):
    k %= SEG
    if k == 0:
        return x
    near = pltpu.roll(x, LANES - k, 1)
    wrapped = pltpu.roll(x, SEG - k, 1)
    return jnp.where(lane_of(x.shape) % SEG < SEG - k, near, wrapped)


def stats_kernel(chunk, rewards, lengths, ids, kept, message, packed, columns, sem):
    rows, width = rewards.shape
    groups = rows // LANES
    tiles = width // LANES
    chunks = rows // chunk

    def fetch(b):
        where = pl.ds(pl.multiple_of(b * chunk, chunk), chunk)
        return pltpu.make_async_copy(rewards.at[where], kept.at[where], sem.at[b])

    for b in range(chunks):
        fetch(b).start()

    both = jnp.concatenate([lengths[...], ids[...]], axis=0).astype(jnp.float32)
    turned = both.T
    owner_row = ids[...] >> 7
    lane = lane_of((LANES, LANES))
    below = lane < lax.broadcasted_iota(jnp.int32, (LANES, LANES), 0)
    sorted_ids = [jnp.zeros((8, LANES), jnp.float32) for _ in range(PARTS)]
    sorted_counts = [jnp.zeros((8, LANES), jnp.float32) for _ in range(PARTS)]
    for g in range(groups):
        length = jnp.broadcast_to(turned[:, g : g + 1], (LANES, LANES))
        prompt = jnp.broadcast_to(turned[:, groups + g : groups + g + 1], (LANES, LANES))
        owner = prompt.astype(jnp.int32) >> 7
        earlier = jnp.where((owner == owner_row[g : g + 1, :]) & below, 1.0, 0.0)
        for h in range(g):
            earlier += jnp.where(owner == owner_row[h : h + 1, :], 1.0, 0.0)
        rank = jnp.sum(earlier, axis=1, keepdims=True)
        slot = owner * SEG + rank.astype(jnp.int32)
        columns[0, g * LANES : (g + 1) * LANES, :] = slot
        columns[1, g * LANES : (g + 1) * LANES, :] = length.astype(jnp.int32)
        for s in range(PARTS):
            here = slot == lane + s * LANES
            sorted_ids[s] += jnp.sum(jnp.where(here, prompt, 0.0).reshape(LANES // 8, 8, LANES), axis=0)
            sorted_counts[s] += jnp.sum(jnp.where(here, length, 0.0).reshape(LANES // 8, 8, LANES), axis=0)

    small_lane = lane_of((chunk, LANES))

    def scan_rows(b):
        where = pl.ds(pl.multiple_of(b * chunk, chunk), chunk)
        left = columns[1, where, :] - small_lane
        shift = kept[where, 0:LANES]
        total = jnp.zeros_like(shift)
        square = jnp.zeros_like(shift)
        for t in range(1, tiles):
            d = kept[where, t * LANES : (t + 1) * LANES] - shift
            if t >= SURE:
                d = jnp.where(left > t * LANES, d, 0.0)
            total += d
            square += d * d
        count = ((left + (LANES - 1)) >> 7).astype(jnp.float32)
        off = total / count
        return shift + off, square - total * off, count

    def join_lanes(b, partial, sums):
        lane_mean, lane_square, count = partial
        where = pl.ds(pl.multiple_of(b * chunk, chunk), chunk)
        length = columns[1, where, :].astype(jnp.float32)
        mean = jnp.sum(lane_mean * count, axis=1, keepdims=True) / length
        away = lane_mean - mean
        square = jnp.sum(lane_square + count * (away * away), axis=1, keepdims=True)
        square = jnp.broadcast_to(square, mean.shape)
        slot = columns[0, where, :]
        result = []
        for s in range(PARTS):
            here = slot == small_lane + s * LANES
            for value, old in ((mean, sums[2 * s]), (square, sums[2 * s + 1])):
                put = jnp.where(here, value, 0.0).reshape(chunk // 8, 8, LANES)
                result.append(old + jnp.sum(put, axis=0))
        return tuple(result)

    zeros = tuple(jnp.zeros((8, LANES), jnp.float32) for _ in range(2 * PARTS))
    fetch(0).wait()
    first = scan_rows(0)

    def step(b, carry):
        partial, sums = carry
        fetch(b).wait()
        current = scan_rows(b)
        return current, join_lanes(b - 1, partial, sums)

    partial, sums = lax.fori_loop(1, chunks, step, (first, zeros))
    sums = join_lanes(chunks - 1, partial, sums)
    lines = []
    for s in range(PARTS):
        for piece in (sorted_ids[s], sorted_counts[s], sums[2 * s], sums[2 * s + 1]):
            lines.append(jnp.sum(piece, axis=0, keepdims=True))
    block = jnp.concatenate(lines, axis=0)
    packed[...] = block
    for peer in range(message.shape[0]):
        message[peer] = block


def own_slots(packed):
    prompt = jnp.concatenate([packed[4 * s % ROWS_MSG : 4 * s % ROWS_MSG + 1, :] for s in range(8)], axis=0)
    mean = jnp.concatenate([packed[4 * s % ROWS_MSG + 2 : 4 * s % ROWS_MSG + 3, :] for s in range(8)], axis=0)
    return prompt, mean


def match_kernel(unroll, heard, packed, found):
    pairs = heard.shape[0] // (2 * ROWS_MSG)
    prompt, mean = own_slots(packed)
    zero = jnp.zeros((8, LANES), jnp.float32)
    totals = [zero, zero, zero]
    batch = 8
    for k0 in range(0, SEG, batch):
        own = [spin(prompt, k) for k in range(k0, k0 + batch)]
        about = [spin(mean, k) for k in range(k0, k0 + batch)]

        def step(i, sums):
            sums = list(sums)
            for u in range(unroll):
                at = (i * unroll + u) * 2 * ROWS_MSG
                pid, count, center, spread = (heard[pl.ds(at + v, 8, stride=VALUES), :] for v in range(VALUES))
                for j in range(batch):
                    same = own[j] == pid
                    n = jnp.where(same, count, 0.0)
                    away = center - about[j]
                    lean = n * away
                    sums[3 * j] += n
                    sums[3 * j + 1] += lean
                    sums[3 * j + 2] += lean * away + jnp.where(same, spread, 0.0)
            return tuple(sums)

        sums = lax.fori_loop(0, pairs // unroll, step, (zero,) * (3 * batch))
        for j in range(batch):
            for v in range(3):
                totals[v] += spin(sums[3 * j + v], -(k0 + j))
    for v in range(3):
        found[v] = totals[v] + pltpu.roll(totals[v], 4, 0)


def apply_kernel(chunk, owner_ref, kept, columns, packed, found_one, found_two, heard_one, heard_two, advantage, mean_out, var_out, staged, table, sem):
    rows, width = kept.shape
    tiles = width // LANES
    chunks = rows // chunk
    small_lane = lane_of((chunk, LANES))
    _, about = own_slots(packed)
    count, lean, square = (found_one[v] + found_two[v] for v in range(3))
    off = lean / count
    var = jnp.maximum(square - lean * off, 0.0) / count
    table[0] = about + off
    table[1] = lax.rsqrt(var + EPSILON)

    def look_up(b):
        where = pl.ds(pl.multiple_of(b * chunk, chunk), chunk)
        slot = columns[0, where, :]
        mean = jnp.zeros((chunk, LANES), jnp.float32)
        scale = jnp.zeros((chunk, LANES), jnp.float32)
        for s in range(PARTS):
            here = slot == small_lane + s * LANES
            mean += jnp.where(here, table[0, s : s + 1, :], 0.0)
            scale += jnp.where(here, table[1, s : s + 1, :], 0.0)
        mean = jnp.sum(mean, axis=1, keepdims=True)
        scale = jnp.sum(scale, axis=1, keepdims=True)
        return jnp.broadcast_to(mean, (chunk, LANES)), jnp.broadcast_to(scale, (chunk, LANES))

    def send(b):
        where = pl.ds(pl.multiple_of(b * chunk, chunk), chunk)
        return pltpu.make_async_copy(staged.at[where], advantage.at[where], sem.at[b])

    def normalize(b, mean, scale):
        where = pl.ds(pl.multiple_of(b * chunk, chunk), chunk)
        left = columns[1, where, :] - small_lane
        for t in range(tiles):
            at = slice(t * LANES, (t + 1) * LANES)
            value = (kept[where, at] - mean) * scale
            if t >= SURE:
                value = jnp.where(left > t * LANES, value, 0.0)
            staged[where, at] = value
        send(b).start()

    def step(b, carry):
        later = look_up(b + 1)
        normalize(b, *carry)
        return later

    last = lax.fori_loop(0, chunks - 1, step, look_up(0))
    normalize(chunks - 1, *last)

    owner = owner_ref[0]
    part, segment = owner // 8, owner % 8
    lane = lane_of((8, LANES))
    place = segment * SEG + lane % SEG
    prompts = (owner * P_DEV + lane).astype(jnp.float32)
    blocks = []
    for heard in (heard_one, heard_two):
        for g in range(heard.shape[0] // (8 * ROWS_MSG)):
            at = g * 8 * ROWS_MSG + part * VALUES
            blocks.append(
                [jnp.take_along_axis(heard[pl.ds(at + v, 8, stride=ROWS_MSG), :], place, axis=1) for v in range(VALUES)]
            )
    zero = jnp.zeros((8, LANES), jnp.float32)
    count_all, sum_all = zero, zero
    for k in range(SEG):
        turned = spin(prompts, k)
        n_k, s_k = zero, zero
        for pid, n, center, _ in blocks:
            n = jnp.where(turned == pid, n, 0.0)
            n_k += n
            s_k += n * center
        count_all += spin(n_k, -k)
        sum_all += spin(s_k, -k)
    count_all = jnp.broadcast_to(jnp.sum(count_all, axis=0, keepdims=True), (8, LANES))
    mean_all = jnp.broadcast_to(jnp.sum(sum_all, axis=0, keepdims=True), (8, LANES)) / count_all
    spread_all = zero
    for k in range(SEG):
        turned = spin(prompts, k)
        about_k = spin(mean_all, k)
        q_k = zero
        for pid, n, center, spread in blocks:
            away = center - about_k
            q_k += jnp.where(turned == pid, spread + n * (away * away), 0.0)
        spread_all += spin(q_k, -k)
    spread_all = jnp.sum(spread_all, axis=0, keepdims=True)
    mean_out[...] = mean_all[0:1, :]
    var_out[...] = spread_all / count_all[0:1, :]

    for b in range(chunks):
        send(b).wait()


def body(rewards, lengths, prompt_ids):
    rows, width = rewards.shape
    groups = rows // LANES
    peers = 1
    for axis in CHIPS:
        peers *= lax.axis_size(axis)
    vmem = pl.BlockSpec(memory_space=pltpu.VMEM)
    hbm = pl.BlockSpec(memory_space=pltpu.HBM)
    chunk = 32
    kept, message, packed, columns = pl.pallas_call(
        lambda *refs: stats_kernel(chunk, *refs),
        out_shape=(
            pltpu.VMEM((rows, width), jnp.float32),
            pltpu.VMEM((peers, ROWS_MSG, LANES), jnp.float32),
            pltpu.VMEM((ROWS_MSG, LANES), jnp.float32),
            pltpu.VMEM((2, rows, LANES), jnp.int32),
        ),
        in_specs=[hbm, vmem, vmem],
        out_specs=(vmem, vmem, vmem, vmem),
        scratch_shapes=[pltpu.SemaphoreType.DMA((rows // chunk,))],
        compiler_params=pltpu.CompilerParams(vmem_limit_bytes=4 * MIB),
        name="row_statistics",
    )(pltpu.with_memory_space_constraint(rewards, pltpu.HBM), lengths.reshape(groups, LANES), prompt_ids.reshape(groups, LANES))

    heard_one = lax.all_to_all(message, CHIPS, 0, 0, tiled=True)
    heard_two = lax.ppermute(heard_one, "dp_2", [(0, 1), (1, 0)])

    def match(heard):
        return pl.pallas_call(
            lambda *refs: match_kernel(2, *refs),
            out_shape=pltpu.VMEM((3, 8, LANES), jnp.float32),
            in_specs=[vmem, vmem],
            out_specs=vmem,
            compiler_params=pltpu.CompilerParams(vmem_limit_bytes=4 * MIB),
            name="match",
        )(heard, packed)

    heard_one = heard_one.reshape(peers * ROWS_MSG, LANES)
    heard_two = heard_two.reshape(peers * ROWS_MSG, LANES)
    found_one = match(heard_one)
    found_two = match(heard_two)
    owner = lax.axis_index(DP).reshape(1).astype(jnp.int32)
    advantage, prompt_mean, prompt_var = pl.pallas_call(
        lambda *refs: apply_kernel(chunk, *refs),
        out_shape=(
            jax.ShapeDtypeStruct((rows, width), jnp.float32),
            jax.ShapeDtypeStruct((1, P_DEV), jnp.float32),
            jax.ShapeDtypeStruct((1, P_DEV), jnp.float32),
        ),
        in_specs=[pl.BlockSpec(memory_space=pltpu.SMEM)] + [vmem] * 7,
        out_specs=(hbm, vmem, vmem),
        scratch_shapes=[
            pltpu.VMEM((rows, width), jnp.float32),
            pltpu.VMEM((2, 8, LANES), jnp.float32),
            pltpu.SemaphoreType.DMA((rows // chunk,)),
        ],
        compiler_params=pltpu.CompilerParams(vmem_limit_bytes=16 * MIB),
        name="normalize",
    )(owner, kept, columns, packed, found_one, found_two, heard_one, heard_two)
    return advantage, prompt_mean.reshape(P_DEV), prompt_var.reshape(P_DEV)


def solution(mesh):
    split = Mesh(mesh.devices.reshape(4, 4, 2, mesh.shape["seq"]), ("dp_0", "dp_1", "dp_2", "seq"))
    placed = (P(DP_SEQ, None), P(DP_SEQ), P(DP_SEQ))
    return jax.shard_map(
        body,
        mesh=split,
        in_specs=placed,
        out_specs=(P(DP_SEQ, None), P(DP), P(DP)),
        check_vma=False,
    )
```

time: 77 us -> 46.6 us (0.61); the launches traced: 75.5 us -> 46.4 us
  matrix products: 19.9 us -> 0 us
  blocking collectives: 40 us -> 23.3 us
  other arithmetic: 13.6 us -> 0 us
  Pallas kernels: 0 us -> 11.5 us
  local copies, waits for them, and re-layouts: 1.19 us -> 8.12 us
  starting transfers between devices: 0 us -> 2.49 us
    all_gather x4 -> x0, blocking collectives: 40 us -> none  [gathered_once(): both, at, found = (lax.all_gather(jnp.concatenate(lines), axis), 0, {})]
    all_to_all x0 -> x1, blocking collectives: none -> 23.3 us  [body(): heard_one = lax.all_to_all(message, CHIPS, 0, 0, tiled=True)]
    dot_general x6 -> x0, matrix products: 19.9 us -> none  [select_dot(): jnp.dot(left, right, precision=lax.Precision.HIGHEST, preferred_element_t...]
    pallas_call x0 -> x4, Pallas kernels: none -> 11.5 us  [the longest x1 4.53 us: body(): pl.pallas_call(lambda *refs: apply_kernel(chunk, *refs), out_shape=(jax.S...]
    unnamed x6 -> x8, local copies, waits for them, and re-layouts: 0.01 us -> 8.12 us
    reduce_sum x2 -> x0, other arithmetic: 7.99 us -> none  [the longest x1 5.8 us: row_statistics(): row_count = jnp.sum(valid.astype(jnp.float32), axis=1)]
    select_n x1 -> x0, other arithmetic: 4.43 us -> none  [body(): jnp.where(valid, (rewards - own_mean[:, None]) * own_scale[:, None], 0.0)]
    ppermute x0 -> x1, starting transfers between devices: none -> 2.49 us  [body(): heard_two = lax.ppermute(heard_one, 'dp_2', [(0, 1), (1, 0)])]
  transfers between devices with their start and end apart: 0 -> 1, of which waited for: 0 -> 1; matrix products, arithmetic and copies ran while one was open for 0% -> 0% of each run, Pallas kernels for 0% -> 3%
where the time goes in v1:
time: 46.6 us; the launch traced here: 46.4 us
  blocking collectives  23.3 us (50%)
  Pallas kernels  11.5 us (25%)
  local copies, waits for them, and re-layouts  8.12 us (17%)
  starting transfers between devices  2.49 us (5%)
  between operations  0.68 us (1%)
    all_to_all x1, blocking collectives, body(): heard_one = lax.all_to_all(message, CHIPS, 0, 0, tiled=True)  23.3 us
    unnamed x8, local copies, waits for them, and re-layouts  8.12 us
    pallas_call x1, Pallas kernels, body(): pl.pallas_call(lambda *refs: apply_kernel(chunk, *refs), out_shape=(jax.S...  4.53 us
    pallas_call x1, Pallas kernels, body(): pl.pallas_call(lambda *refs: stats_kernel(chunk, *refs), out_shape=(pltpu...  4.44 us
    pallas_call x2, Pallas kernels, match(): pl.pallas_call(lambda *refs: match_kernel(2, *refs), out_shape=pltpu.VMEM...  2.5 us
    ppermute x1, starting transfers between devices, body(): heard_two = lax.ppermute(heard_one, 'dp_2', [(0, 1), (1, 0)])  2.49 us
  transfers between devices with their start and end apart: 1, of which 1 were waited for; matrix products, arithmetic and copies ran while one was open for 0% of the time, Pallas kernels for 3%

profile of v1, /device:TPU:1, one launch (start us, length us, event | category | flops | bytes accessed | tf_op | source)
XLA Modules:
  0.0 46.4 jit_solution(5051144569730301406)
XLA Ops:
  0.6 0.0 copy-start.2
  0.6 0.7 %copy-done.2 = s32[512]{0:T(512)S(1)} copy-done((s32[512]{0:T(512)S(1)}, s32[512]{0:T(512)}, u32[]{:S(2)}) %copy-start.2) | copy-done | bytes 2072
  1.3 0.0 copy-start.3
  1.3 0.7 %copy-done.3 = s32[512]{0:T(512)S(1)} copy-done((s32[512]{0:T(512)S(1)}, s32[512]{0:T(512)}, u32[]{:S(2)}) %copy-start.3) | copy-done | bytes 2072
  2.0 4.4 %row_statistics.1 = (f32[512,4096]{1,0:T(8,128)S(1)}, f32[64,16,128]{2,1,0:T(8,128)S(1)}, f32[16,128]{1,0:T(8,128)S(1)}, s32[2,512,128]{2,1,0:T(8,128)S(1)}) custom-call(f32[512,4096]{1,0:T(8,128)} %refs_0_.1, s32[4,128]{1,0:T(4,128)S(1)} %bitcast.11, s32[4,128]{1,0:T(4,128)S(1)} %bitcast.12), custom_call_target="tpu_custom_call" | custom-call | tf_op jit(solution)/shard_map/row_statistics/pallas_call | solution.py:269
  6.4 0.0 copy-start
  6.5 3.4 %copy-done = f32[512,4096]{1,0:T(8,128)} copy-done((f32[512,4096]{1,0:T(8,128)}, f32[512,4096]{1,0:T(8,128)S(1)}, u32[]{:S(2)}) %copy-start) | copy-done | bytes 8388632
  9.8 23.3 %all_to_all.5 = f32[64,16,128]{2,1,0:T(8,128)S(1)} all-to-all(f32[64,16,128]{2,1,0:T(8,128)S(1)} %get-tuple-element.13), channel_id=1, replica_groups=mesh['dp_0'=4,'dp_1'=4,'dp_2'=2,'seq'=4] {'dp_0','dp_1','seq'}, dimensions={0} | all-to-all | bytes 1048576 | tf_op jit(solution)/shard_map/all_to_all | solution.py:284
  33.2 2.5 %collective-permute-start = (f32[64,16,128]{2,1,0:T(8,128)S(1)}, f32[64,16,128]{2,1,0:T(8,128)S(1)}, u32[]{:S(2)}, u32[]{:S(2)}) collective-permute-start(f32[64,16,128]{2,1,0:T(8,128)S(1)} %all_to_all.5), channel_id=1, source_target_pairs={{0,4},{4,0},{1,5},{5,1},{2,6},{6,2},{3,7},{7,3},{8,12},{12,8},{9,1... | collective-permute-start | bytes 1572872 | tf_op jit(solution)/shard_map/ppermute | solution.py:285
  35.7 1.2 %match.2.refs_4_ = f32[3,8,128]{2,1,0:T(8,128)S(1)} custom-call(f32[1024,128]{1,0:T(8,128)S(1)} %bitcast.7, f32[16,128]{1,0:T(8,128)S(1)} %get-tuple-element.12.refs_1_.refs_3_), custom_call_target="tpu_custom_call" | custom-call | tf_op jit(solution)/shard_map/match/pallas_call | solution.py:288
  36.9 0.3 collective-permute-done
  37.2 1.2 %match.3.refs_5_ = f32[3,8,128]{2,1,0:T(8,128)S(1)} custom-call(f32[1024,128]{1,0:T(8,128)S(1)} %bitcast.9, f32[16,128]{1,0:T(8,128)S(1)} %get-tuple-element.12.refs_1_.refs_3_), custom_call_target="tpu_custom_call" | custom-call | tf_op jit(solution)/shard_map/match/pallas_call | solution.py:288
  38.4 0.0 copy-start.1
  38.5 3.4 %copy-done.1 = f32[512,4096]{1,0:T(8,128)S(1)} copy-done((f32[512,4096]{1,0:T(8,128)S(1)}, f32[512,4096]{1,0:T(8,128)}, u32[]{:S(2)}) %copy-start.1) | copy-done | bytes 8388632
  41.8 4.5 %normalize.1 = (f32[512,4096]{1,0:T(8,128)}, f32[1,128]{1,0:T(1,128)}, f32[1,128]{1,0:T(1,128)}) custom-call(s32[1]{0:T(128)} %bitcast.refs_0_, f32[512,4096]{1,0:T(8,128)S(1)} %copy-done.1, s32[2,512,128]{2,1,0:T(8,128)S(1)} %get-tuple-element.11.refs_2_, f32[16,128]{1,0:T(8,128)S(1)} %get-tuple-element.12.refs_1_.refs_3_, f32[3,8,128]{2,1,0:T(8,128)S(1)} %match.2.refs_4_, ...), custom_call_target="tpu_custom_call" | custom-call | tf_op jit(solution)/shard_map/normalize/pallas_call | solution.py:302
Async XLA Ops:
  0.6 0.7 %copy-start.2 = (s32[512]{0:T(512)S(1)}, s32[512]{0:T(512)}, u32[]{:S(2)}) copy-start(s32[512]{0:T(512)} %param.4) | copy-start | bytes 6148
  1.3 0.7 %copy-start.3 = (s32[512]{0:T(512)S(1)}, s32[512]{0:T(512)}, u32[]{:S(2)}) copy-start(s32[512]{0:T(512)} %param.5) | copy-start | bytes 6148
  6.4 3.4 %copy-start = (f32[512,4096]{1,0:T(8,128)}, f32[512,4096]{1,0:T(8,128)S(1)}, u32[]{:S(2)}) copy-start(f32[512,4096]{1,0:T(8,128)S(1)} %get-tuple-element.10.refs_1_) | copy-start | bytes 25165828
  33.2 4.0 %collective-permute-start = (f32[64,16,128]{2,1,0:T(8,128)S(1)}, f32[64,16,128]{2,1,0:T(8,128)S(1)}, u32[]{:S(2)}, u32[]{:S(2)}) collective-permute-start(f32[64,16,128]{2,1,0:T(8,128)S(1)} %all_to_all.5), channel_id=1, source_target_pairs={{0,4},{4,0},{1,5},{5,1},{2,6},{6,2},{3,7},{7,3},{8,12},{12,8},{9,1... | collective-permute-start | bytes 1572872 | tf_op jit(solution)/shard_map/ppermute | solution.py:285
  38.4 3.4 %copy-start.1 = (f32[512,4096]{1,0:T(8,128)S(1)}, f32[512,4096]{1,0:T(8,128)}, u32[]{:S(2)}) copy-start(f32[512,4096]{1,0:T(8,128)} %copy-done) | copy-start | bytes 25165828

commit v2 on v1

--- a/solution.py
+++ b/solution.py
@@ -15,6 +15,7 @@
 CHIPS = ("dp_0", "dp_1", "seq")
 EPSILON = 1e-06
 MIB = 1024 * 1024
+TAG = 8192
 SURE = 4
 
 PARTS = 4
@@ -35,7 +36,7 @@
     return jnp.where(lane_of(x.shape) % SEG < SEG - k, near, wrapped)
 
 
-def stats_kernel(chunk, rewards, lengths, ids, kept, message, packed, columns, sem):
+def stats_kernel(chunk, rewards, lengths_hbm, ids_hbm, kept, message, packed, columns, lengths, ids, sem, small_sem):
     rows, width = rewards.shape
     groups = rows // LANES
     tiles = width // LANES
@@ -45,37 +46,45 @@
         where = pl.ds(pl.multiple_of(b * chunk, chunk), chunk)
         return pltpu.make_async_copy(rewards.at[where], kept.at[where], sem.at[b])
 
-    for b in range(chunks):
+    small = (
+        pltpu.make_async_copy(lengths_hbm, lengths, small_sem.at[0]),
+        pltpu.make_async_copy(ids_hbm, ids, small_sem.at[1]),
+    )
+    for copy in small:
+        copy.start()
+    for b in range(2):
         fetch(b).start()
-
-    both = jnp.concatenate([lengths[...], ids[...]], axis=0).astype(jnp.float32)
-    turned = both.T
-    owner_row = ids[...] >> 7
+    for copy in small:
+        copy.wait()
+    for b in range(2, chunks):
+        fetch(b).start()
+
     lane = lane_of((LANES, LANES))
-    below = lane < lax.broadcasted_iota(jnp.int32, (LANES, LANES), 0)
-    sorted_ids = [jnp.zeros((8, LANES), jnp.float32) for _ in range(PARTS)]
-    sorted_counts = [jnp.zeros((8, LANES), jnp.float32) for _ in range(PARTS)]
+    before = jnp.where(lax.broadcasted_iota(jnp.int32, (LANES, LANES), 0) < lane, 1.0, 0.0)
+    counter = jnp.concatenate([before, jnp.ones((LANES, LANES), jnp.float32)], axis=1)
+    owners = ids[...] >> 7
+    each = lax.broadcasted_iota(jnp.int32, (OWNERS, LANES), 0)
+    mine = [jnp.where(owners[g : g + 1, :] == each, 1.0, 0.0) for g in range(groups)]
+    counts = jnp.dot(jnp.concatenate(mine, axis=0), counter, preferred_element_type=jnp.float32)
+    slots = []
+    so_far = jnp.zeros((OWNERS, LANES), jnp.float32)
     for g in range(groups):
-        length = jnp.broadcast_to(turned[:, g : g + 1], (LANES, LANES))
-        prompt = jnp.broadcast_to(turned[:, groups + g : groups + g + 1], (LANES, LANES))
-        owner = prompt.astype(jnp.int32) >> 7
-        earlier = jnp.where((owner == owner_row[g : g + 1, :]) & below, 1.0, 0.0)
-        for h in range(g):
-            earlier += jnp.where(owner == owner_row[h : h + 1, :], 1.0, 0.0)
-        rank = jnp.sum(earlier, axis=1, keepdims=True)
-        slot = owner * SEG + rank.astype(jnp.int32)
-        columns[0, g * LANES : (g + 1) * LANES, :] = slot
-        columns[1, g * LANES : (g + 1) * LANES, :] = length.astype(jnp.int32)
-        for s in range(PARTS):
-            here = slot == lane + s * LANES
-            sorted_ids[s] += jnp.sum(jnp.where(here, prompt, 0.0).reshape(LANES // 8, 8, LANES), axis=0)
-            sorted_counts[s] += jnp.sum(jnp.where(here, length, 0.0).reshape(LANES // 8, 8, LANES), axis=0)
+        part = counts[g * OWNERS : (g + 1) * OWNERS]
+        rank = jnp.sum(mine[g] * (part[:, :LANES] + so_far), axis=0, keepdims=True)
+        so_far += part[:, LANES:]
+        slots.append(owners[g : g + 1, :] * SEG + rank.astype(jnp.int32))
+    tag = (ids[...] & (P_DEV - 1)) * TAG + lengths[...]
+    turned = jnp.concatenate(slots + [tag], axis=0).astype(jnp.float32).T.astype(jnp.int32)
+    for g in range(groups):
+        at = slice(g * LANES, (g + 1) * LANES)
+        columns[0, at, :] = jnp.broadcast_to(turned[:, g : g + 1], (LANES, LANES))
+        columns[1, at, :] = jnp.broadcast_to(turned[:, groups + g : groups + g + 1], (LANES, LANES))
 
     small_lane = lane_of((chunk, LANES))
 
     def scan_rows(b):
         where = pl.ds(pl.multiple_of(b * chunk, chunk), chunk)
-        left = columns[1, where, :] - small_lane
+        left = (columns[1, where, :] & (TAG - 1)) - small_lane
         shift = kept[where, 0:LANES]
         total = jnp.zeros_like(shift)
         square = jnp.zeros_like(shift)
@@ -92,21 +101,23 @@
     def join_lanes(b, partial, sums):
         lane_mean, lane_square, count = partial
         where = pl.ds(pl.multiple_of(b * chunk, chunk), chunk)
-        length = columns[1, where, :].astype(jnp.float32)
+        tags = columns[1, where, :]
+        length = (tags & (TAG - 1)).astype(jnp.float32)
         mean = jnp.sum(lane_mean * count, axis=1, keepdims=True) / length
         away = lane_mean - mean
         square = jnp.sum(lane_square + count * (away * away), axis=1, keepdims=True)
         square = jnp.broadcast_to(square, mean.shape)
         slot = columns[0, where, :]
-        result = []
+        sums = list(sums)
         for s in range(PARTS):
-            here = slot == small_lane + s * LANES
-            for value, old in ((mean, sums[2 * s]), (square, sums[2 * s + 1])):
-                put = jnp.where(here, value, 0.0).reshape(chunk // 8, 8, LANES)
-                result.append(old + jnp.sum(put, axis=0))
-        return tuple(result)
-
-    zeros = tuple(jnp.zeros((8, LANES), jnp.float32) for _ in range(2 * PARTS))
+            for r in range(0, chunk, 8):
+                row = slice(r, r + 8)
+                here = slot[row] == small_lane[row] + s * LANES
+                for v, value in enumerate((tags, mean, square)):
+                    sums[3 * s + v] = jnp.where(here, value[row], sums[3 * s + v])
+        return tuple(sums)
+
+    zeros = (jnp.zeros((8, LANES), jnp.int32), jnp.zeros((8, LANES), jnp.float32), jnp.zeros((8, LANES), jnp.float32)) * PARTS
     fetch(0).wait()
     first = scan_rows(0)
 
@@ -119,9 +130,11 @@
     partial, sums = lax.fori_loop(1, chunks, step, (first, zeros))
     sums = join_lanes(chunks - 1, partial, sums)
     lines = []
+    one_lane = lane_of((1, LANES))
     for s in range(PARTS):
-        for piece in (sorted_ids[s], sorted_counts[s], sums[2 * s], sums[2 * s + 1]):
-            lines.append(jnp.sum(piece, axis=0, keepdims=True))
+        tags, mean, square = (jnp.sum(piece, axis=0, keepdims=True) for piece in sums[3 * s : 3 * s + 3])
+        prompt = (tags >> 13) + ((s * LANES + one_lane) >> 4) * P_DEV
+        lines += [prompt.astype(jnp.float32), (tags & (TAG - 1)).astype(jnp.float32), mean, square]
     block = jnp.concatenate(lines, axis=0)
     packed[...] = block
     for peer in range(message.shape[0]):
@@ -167,7 +180,7 @@
         found[v] = totals[v] + pltpu.roll(totals[v], 4, 0)
 
 
-def apply_kernel(chunk, owner_ref, kept, columns, packed, found_one, found_two, heard_one, heard_two, advantage, mean_out, var_out, staged, table, sem):
+def apply_kernel(chunk, kept, columns, packed, found_one, found_two, heard_one, heard_two, advantage, mean_out, var_out, staged, table, sem):
     rows, width = kept.shape
     tiles = width // LANES
     chunks = rows // chunk
@@ -198,7 +211,7 @@
 
     def normalize(b, mean, scale):
         where = pl.ds(pl.multiple_of(b * chunk, chunk), chunk)
-        left = columns[1, where, :] - small_lane
+        left = (columns[1, where, :] & (TAG - 1)) - small_lane
         for t in range(tiles):
             at = slice(t * LANES, (t + 1) * LANES)
             value = (kept[where, at] - mean) * scale
@@ -215,7 +228,7 @@
     last = lax.fori_loop(0, chunks - 1, step, look_up(0))
     normalize(chunks - 1, *last)
 
-    owner = owner_ref[0]
+    owner = lax.axis_index(DP)
     part, segment = owner // 8, owner % 8
     lane = lane_of((8, LANES))
     place = segment * SEG + lane % SEG
@@ -257,6 +270,10 @@
         send(b).wait()
 
 
+def in_hbm(x):
+    return pltpu.with_memory_space_constraint(x, pltpu.HBM)
+
+
 def body(rewards, lengths, prompt_ids):
     rows, width = rewards.shape
     groups = rows // LANES
@@ -265,7 +282,7 @@
         peers *= lax.axis_size(axis)
     vmem = pl.BlockSpec(memory_space=pltpu.VMEM)
     hbm = pl.BlockSpec(memory_space=pltpu.HBM)
-    chunk = 32
+    chunk = 64
     kept, message, packed, columns = pl.pallas_call(
         lambda *refs: stats_kernel(chunk, *refs),
         out_shape=(
@@ -274,12 +291,17 @@
             pltpu.VMEM((ROWS_MSG, LANES), jnp.float32),
             pltpu.VMEM((2, rows, LANES), jnp.int32),
         ),
-        in_specs=[hbm, vmem, vmem],
+        in_specs=[hbm, hbm, hbm],
         out_specs=(vmem, vmem, vmem, vmem),
-        scratch_shapes=[pltpu.SemaphoreType.DMA((rows // chunk,))],
+        scratch_shapes=[
+            pltpu.VMEM((groups, LANES), jnp.int32),
+            pltpu.VMEM((groups, LANES), jnp.int32),
+            pltpu.SemaphoreType.DMA((rows // chunk,)),
+            pltpu.SemaphoreType.DMA((2,)),
+        ],
         compiler_params=pltpu.CompilerParams(vmem_limit_bytes=4 * MIB),
         name="row_statistics",
-    )(pltpu.with_memory_space_constraint(rewards, pltpu.HBM), lengths.reshape(groups, LANES), prompt_ids.reshape(groups, LANES))
+    )(in_hbm(rewards), in_hbm(lengths.reshape(groups, LANES)), in_hbm(prompt_ids.reshape(groups, LANES)))
 
     heard_one = lax.all_to_all(message, CHIPS, 0, 0, tiled=True)
     heard_two = lax.ppermute(heard_one, "dp_2", [(0, 1), (1, 0)])
@@ -298,7 +320,6 @@
     heard_two = heard_two.reshape(peers * ROWS_MSG, LANES)
     found_one = match(heard_one)
     found_two = match(heard_two)
-    owner = lax.axis_index(DP).reshape(1).astype(jnp.int32)
     advantage, prompt_mean, prompt_var = pl.pallas_call(
         lambda *refs: apply_kernel(chunk, *refs),
         out_shape=(
@@ -306,7 +327,7 @@
             jax.ShapeDtypeStruct((1, P_DEV), jnp.float32),
             jax.ShapeDtypeStruct((1, P_DEV), jnp.float32),
         ),
-        in_specs=[pl.BlockSpec(memory_space=pltpu.SMEM)] + [vmem] * 7,
+        in_specs=[vmem] * 7,
         out_specs=(hbm, vmem, vmem),
         scratch_shapes=[
             pltpu.VMEM((rows, width), jnp.float32),
@@ -315,7 +336,7 @@
         ],
         compiler_params=pltpu.CompilerParams(vmem_limit_bytes=16 * MIB),
         name="normalize",
-    )(owner, kept, columns, packed, found_one, found_two, heard_one, heard_two)
+    )(kept, columns, packed, found_one, found_two, heard_one, heard_two)
     return advantage, prompt_mean.reshape(P_DEV), prompt_var.reshape(P_DEV)
 
 

time: 46.6 us -> 38.1 us (0.82)
  local copies, waits for them, and re-layouts: 8.12 us -> 0 us
    unnamed x8 -> x0, local copies, waits for them, and re-layouts: 8.12 us -> none
where the time goes in v2:
time: 38.1 us; the launch traced here: 38 us
  blocking collectives  23.3 us (61%)
  Pallas kernels  11.2 us (29%)
  starting transfers between devices  2.49 us (7%)
  between operations  0.65 us (2%)
    all_to_all x1, blocking collectives, body(): heard_one = lax.all_to_all(message, CHIPS, 0, 0, tiled=True)  23.3 us
    pallas_call x1, Pallas kernels, body(): pl.pallas_call(lambda *refs: stats_kernel(chunk, *refs), out_shape=(pltpu...  4.53 us
    pallas_call x1, Pallas kernels, body(): pl.pallas_call(lambda *refs: apply_kernel(chunk, *refs), out_shape=(jax.S...  4.17 us
    pallas_call x2, Pallas kernels, match(): pl.pallas_call(lambda *refs: match_kernel(2, *refs), out_shape=pltpu.VMEM...  2.5 us
    ppermute x1, starting transfers between devices, body(): heard_two = lax.ppermute(heard_one, 'dp_2', [(0, 1), (1, 0)])  2.49 us
  transfers between devices with their start and end apart: 1, of which 1 were waited for; matrix products, arithmetic and copies ran while one was open for 0% of the time, Pallas kernels for 3%

profile of v2, /device:TPU:1, one launch (start us, length us, event | category | flops | bytes accessed | tf_op | source)
XLA Modules:
  0.0 38.0 jit_solution(17859288507118764441)
XLA Ops:
  0.6 4.5 %row_statistics.1 = (f32[512,4096]{1,0:T(8,128)S(1)}, f32[64,16,128]{2,1,0:T(8,128)S(1)}, f32[16,128]{1,0:T(8,128)S(1)}, s32[2,512,128]{2,1,0:T(8,128)S(1)}) custom-call(f32[512,4096]{1,0:T(8,128)} %refs_0_.1, s32[4,128]{1,0:T(4,128)} %bitcast.10, s32[4,128]{1,0:T(4,128)} %bitcast.11), custom_call_target="tpu_custom_call" | custom-call | tf_op jit(solution)/shard_map/row_statistics/pallas_call | solution.py:286
  5.2 23.3 %all_to_all.5 = f32[64,16,128]{2,1,0:T(8,128)S(1)} all-to-all(f32[64,16,128]{2,1,0:T(8,128)S(1)} %get-tuple-element.13), channel_id=1, replica_groups=mesh['dp_0'=4,'dp_1'=4,'dp_2'=2,'seq'=4] {'dp_0','dp_1','seq'}, dimensions={0} | all-to-all | bytes 1048576 | tf_op jit(solution)/shard_map/all_to_all | solution.py:306
  28.5 2.5 %collective-permute-start = (f32[64,16,128]{2,1,0:T(8,128)S(1)}, f32[64,16,128]{2,1,0:T(8,128)S(1)}, u32[]{:S(2)}, u32[]{:S(2)}) collective-permute-start(f32[64,16,128]{2,1,0:T(8,128)S(1)} %all_to_all.5), channel_id=1, source_target_pairs={{0,4},{4,0},{1,5},{5,1},{2,6},{6,2},{3,7},{7,3},{8,12},{12,8},{9,1... | collective-permute-start | bytes 1572872 | tf_op jit(solution)/shard_map/ppermute | solution.py:307
  31.0 1.2 %match.2.refs_3_ = f32[3,8,128]{2,1,0:T(8,128)S(1)} custom-call(f32[1024,128]{1,0:T(8,128)S(1)} %bitcast.6, f32[16,128]{1,0:T(8,128)S(1)} %get-tuple-element.12.refs_1_.refs_2_), custom_call_target="tpu_custom_call" | custom-call | tf_op jit(solution)/shard_map/match/pallas_call | solution.py:310
  32.2 0.3 collective-permute-done
  32.5 1.2 %match.3.refs_4_ = f32[3,8,128]{2,1,0:T(8,128)S(1)} custom-call(f32[1024,128]{1,0:T(8,128)S(1)} %bitcast.8, f32[16,128]{1,0:T(8,128)S(1)} %get-tuple-element.12.refs_1_.refs_2_), custom_call_target="tpu_custom_call" | custom-call | tf_op jit(solution)/shard_map/match/pallas_call | solution.py:310
  33.8 4.2 %normalize.1 = (f32[512,4096]{1,0:T(8,128)}, f32[1,128]{1,0:T(1,128)}, f32[1,128]{1,0:T(1,128)}) custom-call(f32[512,4096]{1,0:T(8,128)S(1)} %get-tuple-element.10.refs_0_, s32[2,512,128]{2,1,0:T(8,128)S(1)} %get-tuple-element.11.refs_1_, f32[16,128]{1,0:T(8,128)S(1)} %get-tuple-element.12.refs_1_.refs_2_, f32[3,8,128]{2,1,0:T(8,128)S(1)} %match.2.refs_3_, ...), custom_call_target="tpu_custom_call" | custom-call | tf_op jit(solution)/shard_map/normalize/pallas_call | solution.py:323
Async XLA Ops:
  28.5 4.0 %collective-permute-start = (f32[64,16,128]{2,1,0:T(8,128)S(1)}, f32[64,16,128]{2,1,0:T(8,128)S(1)}, u32[]{:S(2)}, u32[]{:S(2)}) collective-permute-start(f32[64,16,128]{2,1,0:T(8,128)S(1)} %all_to_all.5), channel_id=1, source_target_pairs={{0,4},{4,0},{1,5},{5,1},{2,6},{6,2},{3,7},{7,3},{8,12},{12,8},{9,1... | collective-permute-start | bytes 1572872 | tf_op jit(solution)/shard_map/ppermute | solution.py:307

commit v3 on v2

--- a/solution.py
+++ b/solution.py
@@ -16,6 +16,8 @@
 EPSILON = 1e-06
 MIB = 1024 * 1024
 TAG = 8192
+TAIL = 16
+HEAD = (16, 16, 32)
 SURE = 4
 
 PARTS = 4
@@ -42,9 +44,17 @@
     tiles = width // LANES
     chunks = rows // chunk
 
-    def fetch(b):
-        where = pl.ds(pl.multiple_of(b * chunk, chunk), chunk)
+    last = (chunk - TAIL, TAIL)
+
+    def fetch(start, count, b):
+        where = pl.ds(start, count)
         return pltpu.make_async_copy(rewards.at[where], kept.at[where], sem.at[b])
+
+    def fetch_chunk(b):
+        return fetch(pl.multiple_of(b * chunk, chunk), chunk, b)
+
+    fetches = [fetch_chunk(b) for b in range(chunks - 1)]
+    fetches += [fetch(rows - chunk, last[0], chunks - 1), fetch(rows - TAIL, TAIL, chunks)]
 
     small = (
         pltpu.make_async_copy(lengths_hbm, lengths, small_sem.at[0]),
@@ -52,12 +62,10 @@
     )
     for copy in small:
         copy.start()
-    for b in range(2):
-        fetch(b).start()
+    for copy in fetches:
+        copy.start(priority=1)
     for copy in small:
         copy.wait()
-    for b in range(2, chunks):
-        fetch(b).start()
 
     lane = lane_of((LANES, LANES))
     before = jnp.where(lax.broadcasted_iota(jnp.int32, (LANES, LANES), 0) < lane, 1.0, 0.0)
@@ -80,11 +88,9 @@
         columns[0, at, :] = jnp.broadcast_to(turned[:, g : g + 1], (LANES, LANES))
         columns[1, at, :] = jnp.broadcast_to(turned[:, groups + g : groups + g + 1], (LANES, LANES))
 
-    small_lane = lane_of((chunk, LANES))
-
-    def scan_rows(b):
-        where = pl.ds(pl.multiple_of(b * chunk, chunk), chunk)
-        left = (columns[1, where, :] & (TAG - 1)) - small_lane
+    def scan_rows(start, count):
+        where = pl.ds(start, count)
+        left = (columns[1, where, :] & (TAG - 1)) - lane_of((count, LANES))
         shift = kept[where, 0:LANES]
         total = jnp.zeros_like(shift)
         square = jnp.zeros_like(shift)
@@ -94,41 +100,49 @@
                 d = jnp.where(left > t * LANES, d, 0.0)
             total += d
             square += d * d
-        count = ((left + (LANES - 1)) >> 7).astype(jnp.float32)
-        off = total / count
-        return shift + off, square - total * off, count
-
-    def join_lanes(b, partial, sums):
-        lane_mean, lane_square, count = partial
-        where = pl.ds(pl.multiple_of(b * chunk, chunk), chunk)
+        number = ((left + (LANES - 1)) >> 7).astype(jnp.float32)
+        off = total / number
+        return shift + off, square - total * off, number
+
+    def join_lanes(start, count, partial, sums):
+        lane_mean, lane_square, number = partial
+        where = pl.ds(start, count)
         tags = columns[1, where, :]
         length = (tags & (TAG - 1)).astype(jnp.float32)
-        mean = jnp.sum(lane_mean * count, axis=1, keepdims=True) / length
+        mean = jnp.sum(lane_mean * number, axis=1, keepdims=True) / length
         away = lane_mean - mean
-        square = jnp.sum(lane_square + count * (away * away), axis=1, keepdims=True)
+        square = jnp.sum(lane_square + number * (away * away), axis=1, keepdims=True)
         square = jnp.broadcast_to(square, mean.shape)
         slot = columns[0, where, :]
+        row_lane = lane_of((8, LANES))
         sums = list(sums)
         for s in range(PARTS):
-            for r in range(0, chunk, 8):
+            for r in range(0, count, 8):
                 row = slice(r, r + 8)
-                here = slot[row] == small_lane[row] + s * LANES
+                here = slot[row] == row_lane + s * LANES
                 for v, value in enumerate((tags, mean, square)):
                     sums[3 * s + v] = jnp.where(here, value[row], sums[3 * s + v])
         return tuple(sums)
 
-    zeros = (jnp.zeros((8, LANES), jnp.int32), jnp.zeros((8, LANES), jnp.float32), jnp.zeros((8, LANES), jnp.float32)) * PARTS
-    fetch(0).wait()
-    first = scan_rows(0)
+    sums = (jnp.zeros((8, LANES), jnp.int32), jnp.zeros((8, LANES), jnp.float32), jnp.zeros((8, LANES), jnp.float32)) * PARTS
+    fetches[0].wait()
+    partial = scan_rows(0, chunk)
 
     def step(b, carry):
         partial, sums = carry
-        fetch(b).wait()
-        current = scan_rows(b)
-        return current, join_lanes(b - 1, partial, sums)
-
-    partial, sums = lax.fori_loop(1, chunks, step, (first, zeros))
-    sums = join_lanes(chunks - 1, partial, sums)
+        start = pl.multiple_of(b * chunk, chunk)
+        fetch_chunk(b).wait()
+        current = scan_rows(start, chunk)
+        return current, join_lanes(pl.multiple_of(start - chunk, chunk), chunk, partial, sums)
+
+    partial, sums = lax.fori_loop(1, chunks - 1, step, (partial, sums))
+    done, size = rows - 2 * chunk, chunk
+    for count, copy in zip(last, fetches[-2:]):
+        copy.wait()
+        current = scan_rows(done + size, count)
+        sums = join_lanes(done, size, partial, sums)
+        partial, done, size = current, done + size, count
+    sums = join_lanes(done, size, partial, sums)
     lines = []
     one_lane = lane_of((1, LANES))
     for s in range(PARTS):
@@ -180,7 +194,7 @@
         found[v] = totals[v] + pltpu.roll(totals[v], 4, 0)
 
 
-def apply_kernel(chunk, kept, columns, packed, found_one, found_two, heard_one, heard_two, advantage, mean_out, var_out, staged, table, sem):
+def apply_kernel(chunk, kept, columns, packed, found_one, found_two, heard_one, heard_two, advantage, mean_out, var_out, staged, table, own, sem, own_sem):
     rows, width = kept.shape
     tiles = width // LANES
     chunks = rows // chunk
@@ -205,28 +219,41 @@
         scale = jnp.sum(scale, axis=1, keepdims=True)
         return jnp.broadcast_to(mean, (chunk, LANES)), jnp.broadcast_to(scale, (chunk, LANES))
 
-    def send(b):
-        where = pl.ds(pl.multiple_of(b * chunk, chunk), chunk)
+    def send(start, count, b):
+        where = pl.ds(start, count)
         return pltpu.make_async_copy(staged.at[where], advantage.at[where], sem.at[b])
 
-    def normalize(b, mean, scale):
-        where = pl.ds(pl.multiple_of(b * chunk, chunk), chunk)
-        left = (columns[1, where, :] & (TAG - 1)) - small_lane
+    def send_chunk(b):
+        return send(pl.multiple_of(b * chunk, chunk), chunk, b)
+
+    def normalize(start, count, mean, scale):
+        where = pl.ds(start, count)
+        left = (columns[1, where, :] & (TAG - 1)) - lane_of((count, LANES))
         for t in range(tiles):
             at = slice(t * LANES, (t + 1) * LANES)
             value = (kept[where, at] - mean) * scale
             if t >= SURE:
                 value = jnp.where(left > t * LANES, value, 0.0)
             staged[where, at] = value
-        send(b).start()
+
+    mean, scale = look_up(0)
+    sent = []
+    at = 0
+    for k, count in enumerate(HEAD):
+        normalize(at, count, mean[at : at + count], scale[at : at + count])
+        sent.append(send(at, count, chunks + k))
+        sent[-1].start()
+        at += count
 
     def step(b, carry):
         later = look_up(b + 1)
-        normalize(b, *carry)
+        normalize(pl.multiple_of(b * chunk, chunk), chunk, *carry)
+        send_chunk(b).start()
         return later
 
-    last = lax.fori_loop(0, chunks - 1, step, look_up(0))
-    normalize(chunks - 1, *last)
+    carry = lax.fori_loop(1, chunks - 1, step, look_up(1))
+    normalize(rows - chunk, chunk, *carry)
+    send_chunk(chunks - 1).start()
 
     owner = lax.axis_index(DP)
     part, segment = owner // 8, owner % 8
@@ -263,11 +290,16 @@
             q_k += jnp.where(turned == pid, spread + n * (away * away), 0.0)
         spread_all += spin(q_k, -k)
     spread_all = jnp.sum(spread_all, axis=0, keepdims=True)
-    mean_out[...] = mean_all[0:1, :]
-    var_out[...] = spread_all / count_all[0:1, :]
-
-    for b in range(chunks):
-        send(b).wait()
+    own[0] = mean_all[0:1, :]
+    own[1] = spread_all / count_all[0:1, :]
+    for k, out in enumerate((mean_out, var_out)):
+        sent.append(pltpu.make_async_copy(own.at[k], out, own_sem.at[k]))
+        sent[-1].start(priority=1)
+
+    for b in range(1, chunks):
+        send_chunk(b).wait()
+    for copy in sent:
+        copy.wait()
 
 
 def in_hbm(x):
@@ -296,19 +328,22 @@
         scratch_shapes=[
             pltpu.VMEM((groups, LANES), jnp.int32),
             pltpu.VMEM((groups, LANES), jnp.int32),
-            pltpu.SemaphoreType.DMA((rows // chunk,)),
+            pltpu.SemaphoreType.DMA((rows // chunk + 1,)),
             pltpu.SemaphoreType.DMA((2,)),
         ],
         compiler_params=pltpu.CompilerParams(vmem_limit_bytes=4 * MIB),
         name="row_statistics",
     )(in_hbm(rewards), in_hbm(lengths.reshape(groups, LANES)), in_hbm(prompt_ids.reshape(groups, LANES)))
 
+    def swap(x):
+        return lax.ppermute(x, "dp_2", [(0, 1), (1, 0)])
+
     heard_one = lax.all_to_all(message, CHIPS, 0, 0, tiled=True)
-    heard_two = lax.ppermute(heard_one, "dp_2", [(0, 1), (1, 0)])
+    heard_two = swap(heard_one)
 
     def match(heard):
         return pl.pallas_call(
-            lambda *refs: match_kernel(2, *refs),
+            lambda *refs: match_kernel(8, *refs),
             out_shape=pltpu.VMEM((3, 8, LANES), jnp.float32),
             in_specs=[vmem, vmem],
             out_specs=vmem,
@@ -323,16 +358,18 @@
     advantage, prompt_mean, prompt_var = pl.pallas_call(
         lambda *refs: apply_kernel(chunk, *refs),
         out_shape=(
-            jax.ShapeDtypeStruct((rows, width), jnp.float32),
-            jax.ShapeDtypeStruct((1, P_DEV), jnp.float32),
-            jax.ShapeDtypeStruct((1, P_DEV), jnp.float32),
+            pltpu.HBM((rows, width), jnp.float32),
+            pltpu.HBM((1, P_DEV), jnp.float32),
+            pltpu.HBM((1, P_DEV), jnp.float32),
         ),
         in_specs=[vmem] * 7,
-        out_specs=(hbm, vmem, vmem),
+        out_specs=(hbm, hbm, hbm),
         scratch_shapes=[
             pltpu.VMEM((rows, width), jnp.float32),
             pltpu.VMEM((2, 8, LANES), jnp.float32),
-            pltpu.SemaphoreType.DMA((rows // chunk,)),
+            pltpu.VMEM((2, 1, LANES), jnp.float32),
+            pltpu.SemaphoreType.DMA((rows // chunk + len(HEAD),)),
+            pltpu.SemaphoreType.DMA((2,)),
         ],
         compiler_params=pltpu.CompilerParams(vmem_limit_bytes=16 * MIB),
         name="normalize",

time: 38.1 us -> 36.9 us (0.969)
  Pallas kernels: 11.2 us -> 9.79 us
    pallas_call x3, Pallas kernels: 6.67 us -> 5.75 us  [the longest x1 3.62 us: body(): pl.pallas_call(lambda *refs: apply_kernel(chunk, *refs), out_shape=(pltpu...]
    pallas_call x1, Pallas kernels: 4.53 us -> 4.04 us  [body(): pl.pallas_call(lambda *refs: stats_kernel(chunk, *refs), out_shape=(pltpu...]
where the time goes in v3:
time: 36.9 us; the launch traced here: 36.7 us
  blocking collectives  23.3 us (63%)
  Pallas kernels  9.79 us (27%)
  starting transfers between devices  2.49 us (7%)
  between operations  0.65 us (2%)
  waiting for transfers between devices  0.46 us (1%)
    all_to_all x1, blocking collectives, body(): heard_one = lax.all_to_all(message, CHIPS, 0, 0, tiled=True)  23.3 us
    pallas_call x1, Pallas kernels, body(): pl.pallas_call(lambda *refs: stats_kernel(chunk, *refs), out_shape=(pltpu...  4.04 us
    pallas_call x1, Pallas kernels, body(): pl.pallas_call(lambda *refs: apply_kernel(chunk, *refs), out_shape=(pltpu...  3.62 us
    ppermute x1, starting transfers between devices, swap(): return lax.ppermute(x, 'dp_2', [(0, 1), (1, 0)])  2.49 us
    pallas_call x2, Pallas kernels, match(): pl.pallas_call(lambda *refs: match_kernel(8, *refs), out_shape=pltpu.VMEM...  2.14 us
  transfers between devices with their start and end apart: 1, of which 1 were waited for; matrix products, arithmetic and copies ran while one was open for 0% of the time, Pallas kernels for 3%

profile of v3, /device:TPU:1, one launch (start us, length us, event | category | flops | bytes accessed | tf_op | source)
XLA Modules:
  0.0 36.7 jit_solution(6259483387585363752)
XLA Ops:
  0.6 4.0 %row_statistics.1 = (f32[512,4096]{1,0:T(8,128)S(1)}, f32[64,16,128]{2,1,0:T(8,128)S(1)}, f32[16,128]{1,0:T(8,128)S(1)}, s32[2,512,128]{2,1,0:T(8,128)S(1)}) custom-call(f32[512,4096]{1,0:T(8,128)} %refs_0_.1, s32[4,128]{1,0:T(4,128)} %bitcast.10, s32[4,128]{1,0:T(4,128)} %bitcast.11), custom_call_target="tpu_custom_call" | custom-call | tf_op jit(solution)/shard_map/row_statistics/pallas_call | solution.py:318
  4.7 23.3 %all_to_all.5 = f32[64,16,128]{2,1,0:T(8,128)S(1)} all-to-all(f32[64,16,128]{2,1,0:T(8,128)S(1)} %get-tuple-element.13), channel_id=1, replica_groups=mesh['dp_0'=4,'dp_1'=4,'dp_2'=2,'seq'=4] {'dp_0','dp_1','seq'}, dimensions={0} | all-to-all | bytes 1048576 | tf_op jit(solution)/shard_map/all_to_all | solution.py:341
  28.0 2.5 %collective-permute-start = (f32[64,16,128]{2,1,0:T(8,128)S(1)}, f32[64,16,128]{2,1,0:T(8,128)S(1)}, u32[]{:S(2)}, u32[]{:S(2)}) collective-permute-start(f32[64,16,128]{2,1,0:T(8,128)S(1)} %all_to_all.5), channel_id=1, source_target_pairs={{0,4},{4,0},{1,5},{5,1},{2,6},{6,2},{3,7},{7,3},{8,12},{12,8},{9,1... | collective-permute-start | bytes 1572872 | tf_op jit(solution)/shard_map/ppermute | solution.py:339
  30.5 1.1 %match.2.refs_3_ = f32[3,8,128]{2,1,0:T(8,128)S(1)} custom-call(f32[1024,128]{1,0:T(8,128)S(1)} %bitcast.6, f32[16,128]{1,0:T(8,128)S(1)} %get-tuple-element.12.refs_1_.refs_2_), custom_call_target="tpu_custom_call" | custom-call | tf_op jit(solution)/shard_map/match/pallas_call | solution.py:345
  31.6 0.5 %collective-permute-done = f32[64,16,128]{2,1,0:T(8,128)S(1)} collective-permute-done((f32[64,16,128]{2,1,0:T(8,128)S(1)}, f32[64,16,128]{2,1,0:T(8,128)S(1)}, u32[]{:S(2)}, u32[]{:S(2)}) %collective-permute-start) | collective-permute-done | bytes 524320 | tf_op jit(solution)/shard_map/ppermute | solution.py:339
  32.0 1.1 %match.3.refs_4_ = f32[3,8,128]{2,1,0:T(8,128)S(1)} custom-call(f32[1024,128]{1,0:T(8,128)S(1)} %bitcast.8, f32[16,128]{1,0:T(8,128)S(1)} %get-tuple-element.12.refs_1_.refs_2_), custom_call_target="tpu_custom_call" | custom-call | tf_op jit(solution)/shard_map/match/pallas_call | solution.py:345
  33.1 3.6 %normalize.1 = (f32[512,4096]{1,0:T(8,128)}, f32[1,128]{1,0:T(1,128)}, f32[1,128]{1,0:T(1,128)}) custom-call(f32[512,4096]{1,0:T(8,128)S(1)} %get-tuple-element.10.refs_0_, s32[2,512,128]{2,1,0:T(8,128)S(1)} %get-tuple-element.11.refs_1_, f32[16,128]{1,0:T(8,128)S(1)} %get-tuple-element.12.refs_1_.refs_2_, f32[3,8,128]{2,1,0:T(8,128)S(1)} %match.2.refs_3_, ...), custom_call_target="tpu_custom_call" | custom-call | tf_op jit(solution)/shard_map/normalize/pallas_call | solution.py:358
Async XLA Ops:
  28.0 4.0 %collective-permute-start = (f32[64,16,128]{2,1,0:T(8,128)S(1)}, f32[64,16,128]{2,1,0:T(8,128)S(1)}, u32[]{:S(2)}, u32[]{:S(2)}) collective-permute-start(f32[64,16,128]{2,1,0:T(8,128)S(1)} %all_to_all.5), channel_id=1, source_target_pairs={{0,4},{4,0},{1,5},{5,1},{2,6},{6,2},{3,7},{7,3},{8,12},{12,8},{9,1... | collective-permute-start | bytes 1572872 | tf_op jit(solution)/shard_map/ppermute | solution.py:339

commit v4 on v3

--- a/solution.py
+++ b/solution.py
@@ -16,6 +16,8 @@
 EPSILON = 1e-06
 MIB = 1024 * 1024
 TAG = 8192
+BATCH = 8
+UNROLL = 8
 TAIL = 16
 HEAD = (16, 16, 32)
 SURE = 4
@@ -161,46 +163,57 @@
     return prompt, mean
 
 
-def match_kernel(unroll, heard, packed, found):
+def match(heard, own, about, sums, first):
     pairs = heard.shape[0] // (2 * ROWS_MSG)
+    zero = jnp.zeros((8, LANES), jnp.float32)
+    for k0 in range(0, SEG, BATCH):
+        ids = [own[k0 + j] for j in range(BATCH)]
+        means = [about[k0 + j] for j in range(BATCH)]
+
+        def step(i, total):
+            total = list(total)
+            for u in range(UNROLL):
+                at = (i * UNROLL + u) * 2 * ROWS_MSG
+                pid, count, center, spread = (heard[pl.ds(at + v, 8, stride=VALUES), :] for v in range(VALUES))
+                for j in range(BATCH):
+                    same = ids[j] == pid
+                    n = jnp.where(same, count, 0.0)
+                    away = center - means[j]
+                    lean = n * away
+                    total[3 * j] += n
+                    total[3 * j + 1] += lean
+                    total[3 * j + 2] += lean * away + jnp.where(same, spread, 0.0)
+            return tuple(total)
+
+        start = (zero,) * (3 * BATCH) if first else tuple(sums[3 * k0 + j] for j in range(3 * BATCH))
+        total = lax.fori_loop(0, pairs // UNROLL, step, start)
+        for j in range(3 * BATCH):
+            sums[3 * k0 + j] = total[j]
+
+
+def match_kernel(heard, packed, own, about, sums):
     prompt, mean = own_slots(packed)
-    zero = jnp.zeros((8, LANES), jnp.float32)
-    totals = [zero, zero, zero]
-    batch = 8
-    for k0 in range(0, SEG, batch):
-        own = [spin(prompt, k) for k in range(k0, k0 + batch)]
-        about = [spin(mean, k) for k in range(k0, k0 + batch)]
-
-        def step(i, sums):
-            sums = list(sums)
-            for u in range(unroll):
-                at = (i * unroll + u) * 2 * ROWS_MSG
-                pid, count, center, spread = (heard[pl.ds(at + v, 8, stride=VALUES), :] for v in range(VALUES))
-                for j in range(batch):
-                    same = own[j] == pid
-                    n = jnp.where(same, count, 0.0)
-                    away = center - about[j]
-                    lean = n * away
-                    sums[3 * j] += n
-                    sums[3 * j + 1] += lean
-                    sums[3 * j + 2] += lean * away + jnp.where(same, spread, 0.0)
-            return tuple(sums)
-
-        sums = lax.fori_loop(0, pairs // unroll, step, (zero,) * (3 * batch))
-        for j in range(batch):
-            for v in range(3):
-                totals[v] += spin(sums[3 * j + v], -(k0 + j))
-    for v in range(3):
-        found[v] = totals[v] + pltpu.roll(totals[v], 4, 0)
-
-
-def apply_kernel(chunk, kept, columns, packed, found_one, found_two, heard_one, heard_two, advantage, mean_out, var_out, staged, table, own, sem, own_sem):
+    for k in range(SEG):
+        own[k] = spin(prompt, k)
+        about[k] = spin(mean, k)
+    match(heard, own, about, sums, True)
+
+
+def more_kernel(heard, own, about, before, sums):
+    sums[...] = before[...]
+    match(heard, own, about, sums, False)
+
+
+def apply_kernel(chunk, kept, columns, packed, own_ids, own_means, sums_one, heard_one, heard_two, heard_last, advantage, mean_out, var_out, staged, sums, table, own, sem, own_sem):
     rows, width = kept.shape
     tiles = width // LANES
     chunks = rows // chunk
     small_lane = lane_of((chunk, LANES))
+    sums[...] = sums_one[...]
+    match(heard_last, own_ids, own_means, sums, False)
     _, about = own_slots(packed)
-    count, lean, square = (found_one[v] + found_two[v] for v in range(3))
+    found = [sum(spin(sums[3 * k + v], -k) for k in range(SEG)) for v in range(3)]
+    count, lean, square = (piece + pltpu.roll(piece, 4, 0) for piece in found)
     off = lean / count
     var = jnp.maximum(square - lean * off, 0.0) / count
     table[0] = about + off
@@ -261,7 +274,7 @@
     place = segment * SEG + lane % SEG
     prompts = (owner * P_DEV + lane).astype(jnp.float32)
     blocks = []
-    for heard in (heard_one, heard_two):
+    for heard in (heard_one, heard_two, heard_last):
         for g in range(heard.shape[0] // (8 * ROWS_MSG)):
             at = g * 8 * ROWS_MSG + part * VALUES
             blocks.append(
@@ -339,22 +352,32 @@
         return lax.ppermute(x, "dp_2", [(0, 1), (1, 0)])
 
     heard_one = lax.all_to_all(message, CHIPS, 0, 0, tiled=True)
-    heard_two = swap(heard_one)
-
-    def match(heard):
-        return pl.pallas_call(
-            lambda *refs: match_kernel(8, *refs),
-            out_shape=pltpu.VMEM((3, 8, LANES), jnp.float32),
-            in_specs=[vmem, vmem],
-            out_specs=vmem,
-            compiler_params=pltpu.CompilerParams(vmem_limit_bytes=4 * MIB),
-            name="match",
-        )(heard, packed)
+    heard_two = swap(heard_one[: peers // 2])
+    heard_last = swap(heard_one[peers // 2 :])
 
     heard_one = heard_one.reshape(peers * ROWS_MSG, LANES)
-    heard_two = heard_two.reshape(peers * ROWS_MSG, LANES)
-    found_one = match(heard_one)
-    found_two = match(heard_two)
+    heard_two = heard_two.reshape(peers // 2 * ROWS_MSG, LANES)
+    heard_last = heard_last.reshape(peers // 2 * ROWS_MSG, LANES)
+    own_ids, own_means, sums = pl.pallas_call(
+        match_kernel,
+        out_shape=(
+            pltpu.VMEM((SEG, 8, LANES), jnp.float32),
+            pltpu.VMEM((SEG, 8, LANES), jnp.float32),
+            pltpu.VMEM((3 * SEG, 8, LANES), jnp.float32),
+        ),
+        in_specs=[vmem, vmem],
+        out_specs=(vmem, vmem, vmem),
+        compiler_params=pltpu.CompilerParams(vmem_limit_bytes=4 * MIB),
+        name="match",
+    )(heard_one, packed)
+    sums = pl.pallas_call(
+        more_kernel,
+        out_shape=pltpu.VMEM((3 * SEG, 8, LANES), jnp.float32),
+        in_specs=[vmem] * 4,
+        out_specs=vmem,
+        compiler_params=pltpu.CompilerParams(vmem_limit_bytes=4 * MIB),
+        name="match_more",
+    )(heard_two, own_ids, own_means, sums)
     advantage, prompt_mean, prompt_var = pl.pallas_call(
         lambda *refs: apply_kernel(chunk, *refs),
         out_shape=(
@@ -362,10 +385,11 @@
             pltpu.HBM((1, P_DEV), jnp.float32),
             pltpu.HBM((1, P_DEV), jnp.float32),
         ),
-        in_specs=[vmem] * 7,
+        in_specs=[vmem] * 9,
         out_specs=(hbm, hbm, hbm),
         scratch_shapes=[
             pltpu.VMEM((rows, width), jnp.float32),
+            pltpu.VMEM((3 * SEG, 8, LANES), jnp.float32),
             pltpu.VMEM((2, 8, LANES), jnp.float32),
             pltpu.VMEM((2, 1, LANES), jnp.float32),
             pltpu.SemaphoreType.DMA((rows // chunk + len(HEAD),)),
@@ -373,7 +397,7 @@
         ],
         compiler_params=pltpu.CompilerParams(vmem_limit_bytes=16 * MIB),
         name="normalize",
-    )(kept, columns, packed, found_one, found_two, heard_one, heard_two)
+    )(kept, columns, packed, own_ids, own_means, sums, heard_one, heard_two, heard_last)
     return advantage, prompt_mean.reshape(P_DEV), prompt_var.reshape(P_DEV)
 
 

time: 36.9 us -> 36.5 us (0.989)
    pallas_call x2, Pallas kernels: 2.14 us -> 1.25 us  [the longest x1 0.87 us: body(): pl.pallas_call(match_kernel, out_shape=(pltpu.VMEM((SEG, 8, LANES), jnp.f...]
    pallas_call x1, Pallas kernels: 3.62 us -> 4.16 us  [body(): pl.pallas_call(lambda *refs: apply_kernel(chunk, *refs), out_shape=(pltpu...]
    ppermute x1 -> x2, starting transfers between devices: 2.49 us -> 2.66 us  [swap(): return lax.ppermute(x, 'dp_2', [(0, 1), (1, 0)])]
  transfers between devices with their start and end apart: 1 -> 2, of which waited for: 1 -> 1; matrix products, arithmetic and copies ran while one was open for 0% -> 0% of each run, Pallas kernels for 3% -> 3%
where the time goes in v4:
time: 36.5 us; the launch traced here: 36.3 us
  blocking collectives  23.3 us (64%)
  Pallas kernels  9.45 us (26%)
  starting transfers between devices  2.66 us (7%)
  between operations  0.66 us (2%)
    all_to_all x1, blocking collectives, body(): heard_one = lax.all_to_all(message, CHIPS, 0, 0, tiled=True)  23.3 us
    pallas_call x1, Pallas kernels, body(): pl.pallas_call(lambda *refs: apply_kernel(chunk, *refs), out_shape=(pltpu...  4.16 us
    pallas_call x1, Pallas kernels, body(): pl.pallas_call(lambda *refs: stats_kernel(chunk, *refs), out_shape=(pltpu...  4.04 us
    ppermute x2, starting transfers between devices, swap(): return lax.ppermute(x, 'dp_2', [(0, 1), (1, 0)])  2.66 us
    pallas_call x1, Pallas kernels, body(): pl.pallas_call(match_kernel, out_shape=(pltpu.VMEM((SEG, 8, LANES), jnp.f...  0.87 us
  transfers between devices with their start and end apart: 2, of which 1 were waited for; matrix products, arithmetic and copies ran while one was open for 0% of the time, Pallas kernels for 3%

profile of v4, /device:TPU:1, one launch (start us, length us, event | category | flops | bytes accessed | tf_op | source)
XLA Modules:
  0.0 36.3 jit_solution(12922187378825518116)
XLA Ops:
  0.6 4.0 %row_statistics.1 = (f32[512,4096]{1,0:T(8,128)S(1)}, f32[64,16,128]{2,1,0:T(8,128)S(1)}, f32[16,128]{1,0:T(8,128)S(1)}, s32[2,512,128]{2,1,0:T(8,128)S(1)}) custom-call(f32[512,4096]{1,0:T(8,128)} %refs_0_.1, s32[4,128]{1,0:T(4,128)} %bitcast.12, s32[4,128]{1,0:T(4,128)} %bitcast.13), custom_call_target="tpu_custom_call" | custom-call | tf_op jit(solution)/shard_map/row_statistics/pallas_call | solution.py:331
  4.7 23.3 %all_to_all.5 = f32[64,16,128]{2,1,0:T(8,128)S(1)} all-to-all(f32[64,16,128]{2,1,0:T(8,128)S(1)} %get-tuple-element.16), channel_id=1, replica_groups=mesh['dp_0'=4,'dp_1'=4,'dp_2'=2,'seq'=4] {'dp_0','dp_1','seq'}, dimensions={0} | all-to-all | bytes 1048576 | tf_op jit(solution)/shard_map/all_to_all | solution.py:354
  28.0 2.6 %collective-permute-start = (f32[32,16,128]{2,1,0:T(8,128)S(1)}, f32[32,16,128]{2,1,0:T(8,128)S(1)}, u32[]{:S(2)}, u32[]{:S(2)}) collective-permute-start(f32[32,16,128]{2,1,0:T(8,128)S(1)} %get-tuple-element.24), channel_id=1, source_target_pairs={{0,4},{4,0},{1,5},{5,1},{2,6},{6,2},{3,7},{7,3},{8,12},{12,8},{9,1... | collective-permute-start | bytes 786440 | tf_op jit(solution)/shard_map/ppermute | solution.py:352
  30.6 0.1 collective-permute-start.1
  30.7 0.9 %match.1 = (f32[16,8,128]{2,1,0:T(8,128)S(1)}, f32[16,8,128]{2,1,0:T(8,128)S(1)}, f32[48,8,128]{2,1,0:T(8,128)S(1)}) custom-call(f32[1024,128]{1,0:T(8,128)S(1)} %bitcast.7, f32[16,128]{1,0:T(8,128)S(1)} %get-tuple-element.15.packed.refs_2_), custom_call_target="tpu_custom_call" | custom-call | tf_op jit(solution)/shard_map/match/pallas_call | solution.py:361
  31.6 0.2 collective-permute-done
  31.8 0.4 %match_more.1.refs_5_ = f32[48,8,128]{2,1,0:T(8,128)S(1)} custom-call(f32[512,128]{1,0:T(8,128)S(1)} %bitcast.9, f32[16,8,128]{2,1,0:T(8,128)S(1)} %get-tuple-element.17.own.refs_3_, f32[16,8,128]{2,1,0:T(8,128)S(1)} %get-tuple-element.18.about.refs_4_, f32[48,8,128]{2,1,0:T(8,128)S(1)} %get-tuple-element.19.before), custom_call_target="tpu_custom_call" | custom-call | tf_op jit(solution)/shard_map/match_more/pallas_call | solution.py:373
  32.2 0.0 collective-permute-done.1
  32.2 4.2 %normalize.1 = (f32[512,4096]{1,0:T(8,128)}, f32[1,128]{1,0:T(1,128)}, f32[1,128]{1,0:T(1,128)}) custom-call(f32[512,4096]{1,0:T(8,128)S(1)} %get-tuple-element.13.refs_0_, s32[2,512,128]{2,1,0:T(8,128)S(1)} %get-tuple-element.14.refs_1_, f32[16,128]{1,0:T(8,128)S(1)} %get-tuple-element.15.packed.refs_2_, f32[16,8,128]{2,1,0:T(8,128)S(1)} %get-tuple-element.17.own.refs_3_, ...), custom_call_target="tpu_custom_call" | custom-call | tf_op jit(solution)/shard_map/normalize/pallas_call | solution.py:381
  (1 shorter events, 0.0 us)
Async XLA Ops:
  28.0 3.7 %collective-permute-start = (f32[32,16,128]{2,1,0:T(8,128)S(1)}, f32[32,16,128]{2,1,0:T(8,128)S(1)}, u32[]{:S(2)}, u32[]{:S(2)}) collective-permute-start(f32[32,16,128]{2,1,0:T(8,128)S(1)} %get-tuple-element.24), channel_id=1, source_target_pairs={{0,4},{4,0},{1,5},{5,1},{2,6},{6,2},{3,7},{7,3},{8,12},{12,8},{9,1... | collective-permute-start | bytes 786440 | tf_op jit(solution)/shard_map/ppermute | solution.py:352
  30.6 1.6 %collective-permute-start.1 = (f32[32,16,128]{2,1,0:T(8,128)S(1)}, f32[32,16,128]{2,1,0:T(8,128)S(1)}, u32[]{:S(2)}, u32[]{:S(2)}) collective-permute-start(f32[32,16,128]{2,1,0:T(8,128)S(1)} %get-tuple-element.23), channel_id=1, source_target_pairs={{0,4},{4,0},{1,5},{5,1},{2,6},{6,2},{3,7},{7,3},{8,12},{12,8},{9,1... | collective-permute-start | bytes 786440 | tf_op jit(solution)/shard_map/ppermute | solution.py:352

commit v5 on v4

--- a/solution.py
+++ b/solution.py
@@ -17,7 +17,7 @@
 MIB = 1024 * 1024
 TAG = 8192
 BATCH = 8
-UNROLL = 8
+UNROLL = 16
 TAIL = 16
 HEAD = (16, 16, 32)
 SURE = 4

time: 36.5 us -> 36.4 us (level)
  no operation moved by 1% of the time
where the time goes in v5:
time: 36.4 us; the launch traced here: 36.2 us
  blocking collectives  23.3 us (64%)
  Pallas kernels  9.32 us (26%)
  starting transfers between devices  2.66 us (7%)
  between operations  0.66 us (2%)
    all_to_all x1, blocking collectives, body(): heard_one = lax.all_to_all(message, CHIPS, 0, 0, tiled=True)  23.3 us
    pallas_call x1, Pallas kernels, body(): pl.pallas_call(lambda *refs: apply_kernel(chunk, *refs), out_shape=(pltpu...  4.1 us
    pallas_call x1, Pallas kernels, body(): pl.pallas_call(lambda *refs: stats_kernel(chunk, *refs), out_shape=(pltpu...  4.04 us
    ppermute x2, starting transfers between devices, swap(): return lax.ppermute(x, 'dp_2', [(0, 1), (1, 0)])  2.66 us
    pallas_call x1, Pallas kernels, body(): pl.pallas_call(match_kernel, out_shape=(pltpu.VMEM((SEG, 8, LANES), jnp.f...  0.84 us
  transfers between devices with their start and end apart: 2, of which 1 were waited for; matrix products, arithmetic and copies ran while one was open for 0% of the time, Pallas kernels for 3%

profile of v5, /device:TPU:1, one launch (start us, length us, event | category | flops | bytes accessed | tf_op | source)
XLA Modules:
  0.0 36.2 jit_solution(8814508608218665435)
XLA Ops:
  0.6 4.0 %row_statistics.1 = (f32[512,4096]{1,0:T(8,128)S(1)}, f32[64,16,128]{2,1,0:T(8,128)S(1)}, f32[16,128]{1,0:T(8,128)S(1)}, s32[2,512,128]{2,1,0:T(8,128)S(1)}) custom-call(f32[512,4096]{1,0:T(8,128)} %refs_0_.1, s32[4,128]{1,0:T(4,128)} %bitcast.12, s32[4,128]{1,0:T(4,128)} %bitcast.13), custom_call_target="tpu_custom_call" | custom-call | tf_op jit(solution)/shard_map/row_statistics/pallas_call | solution.py:331
  4.7 23.3 %all_to_all.5 = f32[64,16,128]{2,1,0:T(8,128)S(1)} all-to-all(f32[64,16,128]{2,1,0:T(8,128)S(1)} %get-tuple-element.16), channel_id=1, replica_groups=mesh['dp_0'=4,'dp_1'=4,'dp_2'=2,'seq'=4] {'dp_0','dp_1','seq'}, dimensions={0} | all-to-all | bytes 1048576 | tf_op jit(solution)/shard_map/all_to_all | solution.py:354
  28.0 2.6 %collective-permute-start = (f32[32,16,128]{2,1,0:T(8,128)S(1)}, f32[32,16,128]{2,1,0:T(8,128)S(1)}, u32[]{:S(2)}, u32[]{:S(2)}) collective-permute-start(f32[32,16,128]{2,1,0:T(8,128)S(1)} %get-tuple-element.24), channel_id=1, source_target_pairs={{0,4},{4,0},{1,5},{5,1},{2,6},{6,2},{3,7},{7,3},{8,12},{12,8},{9,1... | collective-permute-start | bytes 786440 | tf_op jit(solution)/shard_map/ppermute | solution.py:352
  30.6 0.1 collective-permute-start.1
  30.7 0.8 %match.1 = (f32[16,8,128]{2,1,0:T(8,128)S(1)}, f32[16,8,128]{2,1,0:T(8,128)S(1)}, f32[48,8,128]{2,1,0:T(8,128)S(1)}) custom-call(f32[1024,128]{1,0:T(8,128)S(1)} %bitcast.7, f32[16,128]{1,0:T(8,128)S(1)} %get-tuple-element.15.packed.refs_2_), custom_call_target="tpu_custom_call" | custom-call | tf_op jit(solution)/shard_map/match/pallas_call | solution.py:361
  31.6 0.2 collective-permute-done
  31.8 0.3 match_more.1.refs_5_
  32.1 0.0 collective-permute-done.1
  32.1 4.1 %normalize.1 = (f32[512,4096]{1,0:T(8,128)}, f32[1,128]{1,0:T(1,128)}, f32[1,128]{1,0:T(1,128)}) custom-call(f32[512,4096]{1,0:T(8,128)S(1)} %get-tuple-element.13.refs_0_, s32[2,512,128]{2,1,0:T(8,128)S(1)} %get-tuple-element.14.refs_1_, f32[16,128]{1,0:T(8,128)S(1)} %get-tuple-element.15.packed.refs_2_, f32[16,8,128]{2,1,0:T(8,128)S(1)} %get-tuple-element.17.own.refs_3_, ...), custom_call_target="tpu_custom_call" | custom-call | tf_op jit(solution)/shard_map/normalize/pallas_call | solution.py:381
  (1 shorter events, 0.0 us)
Async XLA Ops:
  28.0 3.7 %collective-permute-start = (f32[32,16,128]{2,1,0:T(8,128)S(1)}, f32[32,16,128]{2,1,0:T(8,128)S(1)}, u32[]{:S(2)}, u32[]{:S(2)}) collective-permute-start(f32[32,16,128]{2,1,0:T(8,128)S(1)} %get-tuple-element.24), channel_id=1, source_target_pairs={{0,4},{4,0},{1,5},{5,1},{2,6},{6,2},{3,7},{7,3},{8,12},{12,8},{9,1... | collective-permute-start | bytes 786440 | tf_op jit(solution)/shard_map/ppermute | solution.py:352
  30.6 1.5 %collective-permute-start.1 = (f32[32,16,128]{2,1,0:T(8,128)S(1)}, f32[32,16,128]{2,1,0:T(8,128)S(1)}, u32[]{:S(2)}, u32[]{:S(2)}) collective-permute-start(f32[32,16,128]{2,1,0:T(8,128)S(1)} %get-tuple-element.23), channel_id=1, source_target_pairs={{0,4},{4,0},{1,5},{5,1},{2,6},{6,2},{3,7},{7,3},{8,12},{12,8},{9,1... | collective-permute-start | bytes 786440 | tf_op jit(solution)/shard_map/ppermute | solution.py:352
